TPU v7x, 32 devices: a whole 2x2x4 slice. The times are simulated.
32 devices in a mesh: tx: 8 (over y, x, core), ty: 4 (over z).
Axes of the slice: x: 2, y: 2, z: 4, core: 2. Of those that a mesh axis runs over, the one named last changes fastest.
Arguments:
- adjoint_in: float32 [5, 3, 64, 64, 128], P(None, None, 'ty', 'tx'), may hold values from -6 to 6
- courant: float32 [2, 3, 64, 64, 128], P(None, None, 'ty', 'tx'), may hold values from -0.45 to 0.45
- vertical_inverse: float32 [5, 128, 128], replicated, as said below
- links: int32 [40, 4], replicated, may hold values from 0 to 95, as said below
Outputs:
- adjoint_out: float32 [5, 3, 64, 64, 128], P(None, None, 'ty', 'tx')
Inputs may be any that keep to these rules, and one draw needn't show every extreme that they name: `links`: the three panel slots hold three faces of a cube that meet at one corner, in an order drawn afresh; call them X, Y, Z. X's east side joins Y's west side (code 0, both ways, tile row to same tile row), X's north side joins Z's south side (code 1, both ways, tile column to same tile column), Y's north side joins Z's east side with rotation: cell x = i of Y's top row is the neighbour of cell y = i of Z's east column (code 2 for Z's east ghosts, two rows a tile with off 0 and 8; code 3 for Y's north ghosts, one row a tile with off 0 or 8); all other panel sides are open. Row order is drawn afresh. Offsets are 0 or 8, codes 0 to 3. `vertical_inverse`: each block has a diagonal in [0.6, 1.0) and independent off-diagonal entries.
All inputs are finite; a program needn't handle non-finite values.
Results may differ from a plain program's by a relative error of at most 0.0003.
Values sent between devices are 32-bit elements; how exact they have to be, the bound alone decides.
A program may use at most 64 MiB of HBM per device.

v0:
```python
import jax
import jax.numpy as jnp
from jax import lax
from jax.sharding import PartitionSpec as P

STEPS = 2


def with_halo(block, sides, width):
    for axis, dim in sides:
        count = lax.axis_size(axis)
        forward = [(i, i + 1) for i in range(count - 1)]
        forward.append((count - 1, 0))
        backward = [(target, source) for source, target in forward]
        low = lax.ppermute(
            lax.slice_in_dim(block, block.shape[dim] - width, None, axis=dim), axis, forward
        )
        high = lax.ppermute(lax.slice_in_dim(block, 0, width, axis=dim), axis, backward)
        block = jnp.concatenate([low, block, high], axis=dim)
    return block


def broadcast(block, axis, source):
    block = jnp.where(lax.axis_index(axis) == source, block, jnp.zeros_like(block))
    return lax.psum(block, axis)


def link_tables(links, own_tile, tile_count, slot_count):
    source_slot = links[:, 0] // tile_count
    target_slot = links[:, 1] // tile_count
    target_tile = links[:, 1] % tile_count
    offset = links[:, 2]
    link_kind = links[:, 3]
    slot_ids = jnp.arange(slot_count, dtype=jnp.int32)
    target_hot = (target_slot[:, None] == slot_ids[None, :]).astype(jnp.float32)
    source_hot = (source_slot[:, None] == slot_ids[None, :]).astype(jnp.float32)

    def slot_table(wanted):
        chosen = (
            (target_tile == own_tile) & (link_kind == wanted) & ((link_kind != 2) | (offset == 0))
        )
        weight = chosen.astype(jnp.float32)
        return jnp.sum(
            weight[:, None, None] * target_hot[:, :, None] * source_hot[:, None, :], axis=0
        )

    north_source = jnp.max(jnp.where(link_kind == 2, source_slot, 0))
    east_source = jnp.max(jnp.where(link_kind == 3, source_slot, 0))
    return (slot_table(0), slot_table(1), slot_table(2), slot_table(3), north_source, east_source)


def mix_slots(slot_table, pieces):
    return jnp.sum(slot_table[None, :, :, None, None] * pieces[:, None], axis=2)


def on_device(adjoint_in, courant, vertical_inverse, links):
    col_count = lax.axis_size("tx")
    row_count = lax.axis_size("ty")
    column = lax.axis_index("tx")
    row_index = lax.axis_index("ty")
    slot_count = adjoint_in.shape[1]
    cells_y = adjoint_in.shape[2]
    cells_x = adjoint_in.shape[3]
    tile_count = col_count * row_count
    own_tile = row_index * col_count + column
    x_table, y_table, east_table, north_table, north_source, east_source = link_tables(
        links, own_tile, tile_count, slot_count
    )
    at_east = column == col_count - 1
    at_west = column == 0
    at_north = row_index == row_count - 1
    at_south = row_index == 0
    adjoint = adjoint_in
    for step_index in range(STEPS):
        mixed = jnp.einsum(
            "slm,skyxl->skyxm", vertical_inverse, adjoint, precision=lax.Precision.HIGHEST
        )
        fluxes = courant[:, None] * mixed[None]
        padded = with_halo(fluxes, (("tx", 4), ("ty", 3)), 1)
        halo_east = padded[0, :, :, 1:-1, cells_x + 1]
        halo_west = padded[0, :, :, 1:-1, 0]
        halo_north = padded[1, :, :, cells_y + 1, 1:-1]
        halo_south = padded[1, :, :, 0, 1:-1]
        top_rows = lax.dynamic_slice_in_dim(fluxes[1, :, :, cells_y - 1], north_source, 1, 1)
        east_cols = lax.dynamic_slice_in_dim(fluxes[0, :, :, :, cells_x - 1], east_source, 1, 1)
        north_below = broadcast(top_rows, "ty", row_count - 1)
        north_whole = lax.all_gather(north_below, "tx", axis=2, tiled=True)
        east_beside = broadcast(east_cols, "tx", col_count - 1)
        east_whole = lax.all_gather(east_beside, "ty", axis=2, tiled=True)
        north_piece = lax.dynamic_slice_in_dim(north_whole, row_index * cells_y, cells_y, 2)
        east_piece = lax.dynamic_slice_in_dim(east_whole, column * cells_x, cells_x, 2)
        rotated_east = -jnp.sum(east_table, axis=1)[None, :, None, None] * north_piece
        rotated_north = -jnp.sum(north_table, axis=1)[None, :, None, None] * east_piece
        ghost_east = jnp.where(at_east, mix_slots(x_table, halo_east) + rotated_east, halo_east)
        ghost_west = jnp.where(at_west, mix_slots(x_table, halo_west), halo_west)
        ghost_north = jnp.where(
            at_north, mix_slots(y_table, halo_north) + rotated_north, halo_north
        )
        ghost_south = jnp.where(at_south, mix_slots(y_table, halo_south), halo_south)
        x_line = jnp.concatenate(
            [ghost_west[:, :, :, None], fluxes[0], ghost_east[:, :, :, None]], axis=3
        )
        y_line = jnp.concatenate(
            [ghost_south[:, :, None], fluxes[1], ghost_north[:, :, None]], axis=2
        )
        adjoint = (
            mixed
            + 0.5 * (x_line[:, :, :, 2:] - x_line[:, :, :, :-2])
            + 0.5 * (y_line[:, :, 2:] - y_line[:, :, :-2])
        )
    return adjoint


def solution(mesh):
    placed = (P(None, None, "ty", "tx", None), P(None, None, "ty", "tx", None), P(), P())
    return jax.shard_map(
        on_device,
        mesh=mesh,
        in_specs=placed,
        out_specs=P(None, None, "ty", "tx", None),
        check_vma=False,
    )
```

profile of v0, /device:TPU:0, one launch (start us, length us, event | category | flops | bytes accessed | tf_op | source)
XLA Modules:
  0.0 178.6 jit_solution(6658720027340490278)
XLA Ops:
  0.0 1.2 copy.186
  1.3 1.9 %fusion.13 = f32[5,3,16,8,128]{4,3,2,1,0:T(8,128)S(1)} fusion(f32[5,3,16,8,128]{4,3,2,1,0:T(8,128)S(1)} %copy-done, f32[5,128,128]{2,1,0:T(8,128)} %param.6), kind=kOutput, calls=%fused_computation.33 | convolution fusion | flops 377487360 | bytes 2293760 | tf_op jit(solution)/shard_map/slm,skyxl->skyxm/dot_general | solution.py:75
  3.3 0.9 copy-done.1
  5.9 2.9 %collective-permute-start = (f32[2,5,3,16,1,128]{5,3,2,1,4,0:T(8,128)}, f32[2,5,3,16,1,128]{5,3,2,1,4,0:T(8,128)}, u32[]{:S(2)}, u32[]{:S(2)}) collective-permute-start(f32[2,5,3,16,1,128]{5,3,2,1,4,0:T(8,128)} %get-tuple-element.33), channel_id=1, source_target_pairs={{4,0},{8,4},{12,8},{16,12},{20,16},{24,20},{28,24},{0,28},{5,1},{9... | collective-permute-start | bytes 737288 | tf_op jit(solution)/shard_map/ppermute | solution.py:18
  14.3 20.5 %psum.28 = f32[5,1,8,128]{3,2,0,1:T(8,128)} all-reduce(f32[5,1,8,128]{3,2,0,1:T(8,128)S(1)} %bitcast.157), channel_id=1, replica_groups=mesh['tx'=8,'ty'=4] {'ty'}, use_global_device_ids=true, to_apply=%region_4.5 | all-reduce | flops 5120 | bytes 40960 | tf_op jit(solution)/shard_map/psum | solution.py:25
  35.5 22.7 %psum.29 = f32[5,1,16,128]{3,2,0,1:T(8,128)S(1)} all-reduce(f32[5,1,16,128]{3,2,0,1:T(8,128)S(1)} %select_bitcast_fusion.1), channel_id=1, replica_groups=mesh['tx'=8,'ty'=4] {'tx'}, use_global_device_ids=true, to_apply=%region_10.11 | all-reduce | flops 10240 | bytes 81920 | tf_op jit(solution)/shard_map/psum | solution.py:25
  58.3 13.5 %all_gather.13 = f32[5,1,64,128]{3,2,0,1:T(8,128)S(1)} all-gather(f32[5,1,16,128]{3,2,0,1:T(8,128)S(1)} %psum.29), channel_id=1, replica_groups=mesh['tx'=8,'ty'=4] {'ty'}, dimensions={2}, use_global_device_ids=true | all-gather | bytes 204800 | tf_op jit(solution)/shard_map/all_gather | solution.py:89
  71.7 9.5 %all_gather.12 = f32[5,1,64,128]{3,2,0,1:T(8,128)S(1)} all-gather(f32[5,1,8,128]{3,2,0,1:T(8,128)} %psum.28), channel_id=1, replica_groups=mesh['tx'=8,'ty'=4] {'tx'}, dimensions={2}, use_global_device_ids=true | all-gather | bytes 184320 | tf_op jit(solution)/shard_map/all_gather | solution.py:87
  81.4 1.3 pad_maximum_fusion.13
  82.8 1.9 %collective-permute-start.3 = (f32[2,5,3,1,10,128]{5,3,2,1,4,0:T(1,128)S(1)}, f32[2,5,3,1,10,128]{5,3,2,1,4,0:T(1,128)S(1)}, u32[]{:S(2)}, u32[]{:S(2)}) collective-permute-start(f32[2,5,3,1,10,128]{5,3,2,1,4,0:T(1,128)S(1)} %get-tuple-element.25), channel_id=1, source_target_pairs={{0,1},{1,2},{2,3},{3,0},{4,5},{5,6},{6,7},{7,4},{8,9},{9,10},{10,1... | collective-permute-start | bytes 460808 | tf_op jit(solution)/shard_map/ppermute | solution.py:15
  86.7 1.0 bitcast_select_fusion.2
  89.5 2.8 %collective-permute-done.3 = f32[2,5,3,1,10,128]{5,3,2,1,4,0:T(1,128)S(1)} collective-permute-done((f32[2,5,3,1,10,128]{5,3,2,1,4,0:T(1,128)S(1)}, f32[2,5,3,1,10,128]{5,3,2,1,4,0:T(1,128)S(1)}, u32[]{:S(2)}, u32[]{:S(2)}) %collective-permute-start.3) | collective-permute-done | bytes 153632 | tf_op jit(solution)/shard_map/ppermute | solution.py:15
  93.0 1.7 fusion.9
  96.6 1.4 slice_bitcast_fusion
  98.1 23.2 %psum.31 = f32[5,1,16,128]{3,2,0,1:T(8,128)S(1)} all-reduce(f32[5,1,16,128]{3,2,0,1:T(8,128)S(1)} %select_bitcast_fusion), channel_id=1, replica_groups=mesh['tx'=8,'ty'=4] {'tx'}, use_global_device_ids=true, to_apply=%region_16.17 | all-reduce | flops 10240 | bytes 81920 | tf_op jit(solution)/shard_map/psum | solution.py:25
  121.3 13.4 %all_gather.15 = f32[5,1,64,128]{3,2,0,1:T(8,128)S(1)} all-gather(f32[5,1,16,128]{3,2,0,1:T(8,128)S(1)} %psum.31), channel_id=1, replica_groups=mesh['tx'=8,'ty'=4] {'ty'}, dimensions={2}, use_global_device_ids=true | all-gather | bytes 204800 | tf_op jit(solution)/shard_map/all_gather | solution.py:89
  134.7 2.6 %collective-permute-start.4 = (f32[2,5,3,16,1,128]{5,3,2,1,4,0:T(8,128)}, f32[2,5,3,16,1,128]{5,3,2,1,4,0:T(8,128)S(1)}, u32[]{:S(2)}, u32[]{:S(2)}) collective-permute-start(f32[2,5,3,16,1,128]{5,3,2,1,4,0:T(8,128)} %get-tuple-element.29), channel_id=1, source_target_pairs={{4,0},{8,4},{12,8},{16,12},{20,16},{24,20},{28,24},{0,28},{5,1},{9... | collective-permute-start | bytes 737288 | tf_op jit(solution)/shard_map/ppermute | solution.py:18
  137.4 2.5 %copy.252 = f32[1,5,3,16,8,128]{5,4,3,2,1,0:T(8,128)} copy(f32[1,5,3,16,8,128]{5,3,2,1,4,0:T(8,128)} %get-tuple-element.27) | data formatting | bytes 1966080 | tf_op jit(solution)/shard_map/slice | solution.py:101
  139.9 17.6 %psum.30 = f32[5,1,8,128]{3,2,0,1:T(8,128)S(1)} all-reduce(f32[5,1,8,128]{3,2,0,1:T(8,128)S(1)} %bitcast.156), channel_id=1, replica_groups=mesh['tx'=8,'ty'=4] {'ty'}, use_global_device_ids=true, to_apply=%region_13.14 | all-reduce | flops 5120 | bytes 40960 | tf_op jit(solution)/shard_map/psum | solution.py:25
  157.5 8.7 %all_gather.14 = f32[5,1,64,128]{3,2,0,1:T(8,128)S(1)} all-gather(f32[5,1,8,128]{3,2,0,1:T(8,128)S(1)} %psum.30), channel_id=1, replica_groups=mesh['tx'=8,'ty'=4] {'tx'}, dimensions={2}, use_global_device_ids=true | all-gather | bytes 184320 | tf_op jit(solution)/shard_map/all_gather | solution.py:87
  166.5 2.0 %collective-permute-start.7 = (f32[2,5,3,1,10,128]{5,3,2,1,4,0:T(1,128)S(1)}, f32[2,5,3,1,10,128]{5,3,2,1,4,0:T(1,128)S(1)}, u32[]{:S(2)}, u32[]{:S(2)}) collective-permute-start(f32[2,5,3,1,10,128]{5,3,2,1,4,0:T(1,128)S(1)} %get-tuple-element.23), channel_id=1, source_target_pairs={{0,1},{1,2},{2,3},{3,0},{4,5},{5,6},{6,7},{7,4},{8,9},{9,10},{10,1... | collective-permute-start | bytes 460808 | tf_op jit(solution)/shard_map/ppermute | solution.py:15
  168.8 4.4 %collective-permute-done.6 = f32[2,5,3,1,10,128]{5,3,2,1,4,0:T(1,128)S(1)} collective-permute-done((f32[2,5,3,1,10,128]{5,3,2,1,4,0:T(1,128)S(1)}, f32[2,5,3,1,10,128]{5,3,2,1,4,0:T(1,128)S(1)}, u32[]{:S(2)}, u32[]{:S(2)}) %collective-permute-start.6) | collective-permute-done | bytes 153632 | tf_op jit(solution)/shard_map/ppermute | solution.py:18
  173.3 2.8 %collective-permute-done.7 = f32[2,5,3,1,10,128]{5,3,2,1,4,0:T(1,128)S(1)} collective-permute-done((f32[2,5,3,1,10,128]{5,3,2,1,4,0:T(1,128)S(1)}, f32[2,5,3,1,10,128]{5,3,2,1,4,0:T(1,128)S(1)}, u32[]{:S(2)}, u32[]{:S(2)}) %collective-permute-start.7) | collective-permute-done | bytes 153632 | tf_op jit(solution)/shard_map/ppermute | solution.py:15
  176.8 1.8 fusion.4
  (90 shorter events, 11.7 us)
Async XLA Ops:
  0.0 1.3 copy-start
  3.3 0.9 copy-start.1
  4.4 4.3 %copy-start.8 = (s32[40,4]{0,1:T(4,128)S(1)}, s32[40,4]{0,1:T(4,128)}, u32[]{:S(2)}) copy-start(s32[40,4]{0,1:T(4,128)} %param.7) | copy-start | bytes 1924
  5.4 75.9 %collective-permute-start.1 = (f32[2,5,3,16,1,128]{5,3,2,1,4,0:T(8,128)}, f32[2,5,3,16,1,128]{5,3,2,1,4,0:T(8,128)}, u32[]{:S(2)}, u32[]{:S(2)}) collective-permute-start(f32[2,5,3,16,1,128]{5,3,2,1,4,0:T(8,128)} %get-tuple-element.32), channel_id=1, source_target_pairs={{0,4},{4,8},{8,12},{12,16},{16,20},{20,24},{24,28},{28,0},{1,5},{5... | collective-permute-start | bytes 737288 | tf_op jit(solution)/shard_map/ppermute | solution.py:15
  5.9 75.5 %collective-permute-start = (f32[2,5,3,16,1,128]{5,3,2,1,4,0:T(8,128)}, f32[2,5,3,16,1,128]{5,3,2,1,4,0:T(8,128)}, u32[]{:S(2)}, u32[]{:S(2)}) collective-permute-start(f32[2,5,3,16,1,128]{5,3,2,1,4,0:T(8,128)} %get-tuple-element.33), channel_id=1, source_target_pairs={{4,0},{8,4},{12,8},{16,12},{20,16},{24,20},{28,24},{0,28},{5,1},{9... | collective-permute-start | bytes 737288 | tf_op jit(solution)/shard_map/ppermute | solution.py:18
  81.3 5.4 %copy-start.10 = (f32[3]{0:T(128)S(1)}, f32[3]{0:T(128)}, u32[]{:S(2)}) copy-start(f32[3]{0:T(128)} %neg.18) | copy-start | bytes 40
  82.7 6.8 %collective-permute-start.2 = (f32[2,5,3,1,10,128]{5,3,2,1,4,0:T(1,128)S(1)}, f32[2,5,3,1,10,128]{5,3,2,1,4,0:T(1,128)S(1)}, u32[]{:S(2)}, u32[]{:S(2)}) collective-permute-start(f32[2,5,3,1,10,128]{5,3,2,1,4,0:T(1,128)S(1)} %get-tuple-element.24), channel_id=1, source_target_pairs={{1,0},{2,1},{3,2},{0,3},{5,4},{6,5},{7,6},{4,7},{9,8},{10,9},{11,1... | collective-permute-start | bytes 460808 | tf_op jit(solution)/shard_map/ppermute | solution.py:18
  82.8 9.5 %collective-permute-start.3 = (f32[2,5,3,1,10,128]{5,3,2,1,4,0:T(1,128)S(1)}, f32[2,5,3,1,10,128]{5,3,2,1,4,0:T(1,128)S(1)}, u32[]{:S(2)}, u32[]{:S(2)}) collective-permute-start(f32[2,5,3,1,10,128]{5,3,2,1,4,0:T(1,128)S(1)} %get-tuple-element.25), channel_id=1, source_target_pairs={{0,1},{1,2},{2,3},{3,0},{4,5},{5,6},{6,7},{7,4},{8,9},{9,10},{10,1... | collective-permute-start | bytes 460808 | tf_op jit(solution)/shard_map/ppermute | solution.py:15
  86.7 5.9 %copy-start.9 = (f32[3]{0:T(128)S(1)}, f32[3]{0:T(128)}, u32[]{:S(2)}) copy-start(f32[3]{0:T(128)} %neg.19) | copy-start | bytes 40
  88.7 4.3 %copy-start.2 = (f32[5,3,16,8,128]{4,3,2,1,0:T(8,128)S(1)}, f32[5,3,16,8,128]{4,3,2,1,0:T(8,128)}, u32[]{:S(2)}) copy-start(f32[5,3,16,8,128]{4,3,2,1,0:T(8,128)} %copy-done.1) | copy-start | bytes 2949124
  88.8 4.3 %copy-start.7 = (f32[5,128,128]{2,1,0:T(8,128)S(1)}, f32[5,128,128]{2,1,0:T(8,128)}, u32[]{:S(2)}) copy-start(f32[5,128,128]{2,1,0:T(8,128)} %param.6) | copy-start | bytes 983044
  94.8 0.9 copy-start.3
  134.7 31.5 %collective-permute-start.5 = (f32[2,5,3,16,1,128]{5,3,2,1,4,0:T(8,128)}, f32[2,5,3,16,1,128]{5,3,2,1,4,0:T(8,128)S(1)}, u32[]{:S(2)}, u32[]{:S(2)}) collective-permute-start(f32[2,5,3,16,1,128]{5,3,2,1,4,0:T(8,128)} %get-tuple-element.28), channel_id=1, source_target_pairs={{0,4},{4,8},{8,12},{12,16},{16,20},{20,24},{24,28},{28,0},{1,5},{5... | collective-permute-start | bytes 737288 | tf_op jit(solution)/shard_map/ppermute | solution.py:15
  134.7 31.5 %collective-permute-start.4 = (f32[2,5,3,16,1,128]{5,3,2,1,4,0:T(8,128)}, f32[2,5,3,16,1,128]{5,3,2,1,4,0:T(8,128)S(1)}, u32[]{:S(2)}, u32[]{:S(2)}) collective-permute-start(f32[2,5,3,16,1,128]{5,3,2,1,4,0:T(8,128)} %get-tuple-element.29), channel_id=1, source_target_pairs={{4,0},{8,4},{12,8},{16,12},{20,16},{24,20},{28,24},{0,28},{5,1},{9... | collective-permute-start | bytes 737288 | tf_op jit(solution)/shard_map/ppermute | solution.py:18
  166.4 10.1 %copy-start.5 = (f32[5,3,16,8,128]{4,2,1,0,3:T(8,128)S(1)}, f32[5,3,16,8,128]{4,2,1,0,3:T(8,128)}, u32[]{:S(2)}) copy-start(f32[5,3,16,8,128]{4,2,1,0,3:T(8,128)} %get-tuple-element.26) | copy-start | bytes 2949124
  166.4 6.8 %collective-permute-start.6 = (f32[2,5,3,1,10,128]{5,3,2,1,4,0:T(1,128)S(1)}, f32[2,5,3,1,10,128]{5,3,2,1,4,0:T(1,128)S(1)}, u32[]{:S(2)}, u32[]{:S(2)}) collective-permute-start(f32[2,5,3,1,10,128]{5,3,2,1,4,0:T(1,128)S(1)} %get-tuple-element.22), channel_id=1, source_target_pairs={{1,0},{2,1},{3,2},{0,3},{5,4},{6,5},{7,6},{4,7},{9,8},{10,9},{11,1... | collective-permute-start | bytes 460808 | tf_op jit(solution)/shard_map/ppermute | solution.py:18
  166.5 9.6 %collective-permute-start.7 = (f32[2,5,3,1,10,128]{5,3,2,1,4,0:T(1,128)S(1)}, f32[2,5,3,1,10,128]{5,3,2,1,4,0:T(1,128)S(1)}, u32[]{:S(2)}, u32[]{:S(2)}) collective-permute-start(f32[2,5,3,1,10,128]{5,3,2,1,4,0:T(1,128)S(1)} %get-tuple-element.23), channel_id=1, source_target_pairs={{0,1},{1,2},{2,3},{3,0},{4,5},{5,6},{6,7},{7,4},{8,9},{9,10},{10,1... | collective-permute-start | bytes 460808 | tf_op jit(solution)/shard_map/ppermute | solution.py:15
  168.8 8.0 %copy-start.4 = (f32[5,3,16,8,128]{4,3,2,1,0:T(8,128)S(1)}, f32[5,3,16,8,128]{4,3,2,1,0:T(8,128)}, u32[]{:S(2)}) copy-start(f32[5,3,16,8,128]{4,3,2,1,0:T(8,128)} %copy-done.3) | copy-start | bytes 2949124
  168.8 8.0 %copy-start.6 = (f32[1,5,3,16,8,128]{5,4,3,2,1,0:T(8,128)S(1)}, f32[1,5,3,16,8,128]{5,4,3,2,1,0:T(8,128)}, u32[]{:S(2)}) copy-start(f32[1,5,3,16,8,128]{5,4,3,2,1,0:T(8,128)} %copy.252) | copy-start | bytes 2949124
where the time goes:
time: 179 us
  blocking collectives  129 us (72%)
  local copies, waits for them, and re-layouts  11.1 us (6%)
  waiting for transfers between devices  10.7 us (6%)
  starting transfers between devices  10.1 us (6%)
  other arithmetic  9.29 us (5%)
  between operations  4.59 us (3%)
  matrix products  3.63 us (2%)
    psum x4, blocking collectives, broadcast(): return lax.psum(block, axis)  84 us
    all_gather x2, blocking collectives, on_device(): east_whole = lax.all_gather(east_beside, 'ty', axis=2, tiled=True)  26.9 us
    all_gather x2, blocking collectives, on_device(): north_whole = lax.all_gather(north_below, 'tx', axis=2, tiled=True)  18.2 us
    ppermute x4, starting transfers between devices, with_halo(): lax.ppermute(lax.slice_in_dim(block, 0, width, axis=dim), axis, backward)  5.73 us
    ppermute x4, waiting for transfers between devices, with_halo(): lax.ppermute(lax.slice_in_dim(block, block.shape[dim] - width, None, axis...  5.56 us
    ppermute x4, waiting for transfers between devices, with_halo(): lax.ppermute(lax.slice_in_dim(block, 0, width, axis=dim), axis, backward)  5.12 us
    ppermute x4, starting transfers between devices, with_halo(): lax.ppermute(lax.slice_in_dim(block, block.shape[dim] - width, None, axis...  4.4 us
    dot_general x2, matrix products, on_device(): jnp.einsum('slm,skyxl->skyxm', vertical_inverse, adjoint, precision=lax.P...  3.63 us
  transfers between devices with their start and end apart: 8, of which 4 were waited for; matrix products, arithmetic and copies ran while one was open for 5% of the time, Pallas kernels for 0%

commit v1 on v0

--- a/solution.py
+++ b/solution.py
@@ -86,7 +86,23 @@
         north_below = broadcast(top_rows, "ty", row_count - 1)
         north_whole = lax.all_gather(north_below, "tx", axis=2, tiled=True)
         east_beside = broadcast(east_cols, "tx", col_count - 1)
-        east_whole = lax.all_gather(east_beside, "ty", axis=2, tiled=True)
+
+        def _turn_lane(mine_x, dimension_no):
+            o_now = lax.axis_index("ty")
+            all_values = lax.axis_size("ty")
+            e_next, t1 = (all_values, o_now)
+            carry_out, step_out = (mine_x, 1)
+            while step_out < e_next:
+                mid_arr = lax.ppermute(
+                    carry_out, "ty", [(dd, dd ^ step_out) for dd in range(e_next)]
+                )
+                v_next = jnp.concatenate([carry_out, mid_arr], dimension_no)
+                g_now = jnp.concatenate([mid_arr, carry_out], dimension_no)
+                carry_out = jnp.where(t1 & step_out == 0, v_next, g_now)
+                step_out = 2 * step_out
+            return carry_out
+
+        east_whole = _turn_lane(east_beside, 2)
         north_piece = lax.dynamic_slice_in_dim(north_whole, row_index * cells_y, cells_y, 2)
         east_piece = lax.dynamic_slice_in_dim(east_whole, column * cells_x, cells_x, 2)
         rotated_east = -jnp.sum(east_table, axis=1)[None, :, None, None] * north_piece

time: 179 us -> 170 us (0.950)
  blocking collectives: 129 us -> 102 us
  waiting for transfers between devices: 10.7 us -> 18.1 us
  other arithmetic: 9.29 us -> 15.1 us
  starting transfers between devices: 10.1 us -> 13.1 us
    all_gather x2 -> x0, blocking collectives: 26.9 us -> none  [on_device(): east_whole = lax.all_gather(east_beside, 'ty', axis=2, tiled=True)]
    ppermute x0 -> x4, waiting for transfers between devices: none -> 8.67 us  [_turn_lane(): lax.ppermute(carry_out, 'ty', [(dd, dd ^ step_out) for dd in range(e_next)])]
    ppermute x0 -> x4, starting transfers between devices: none -> 3.1 us  [_turn_lane(): lax.ppermute(carry_out, 'ty', [(dd, dd ^ step_out) for dd in range(e_next)])]
    ppermute x4, starting transfers between devices: 4.4 us -> 2.42 us  [with_halo(): lax.ppermute(lax.slice_in_dim(block, block.shape[dim] - width, None, axis...]
    ppermute x4, starting transfers between devices: 5.73 us -> 7.61 us  [with_halo(): lax.ppermute(lax.slice_in_dim(block, 0, width, axis=dim), axis, backward)]
    unnamed x23 -> x33, local copies, waits for them, and re-layouts: 2.87 us -> 4.02 us
  transfers between devices with their start and end apart: 8 -> 12, of which waited for: 4 -> 6; matrix products, arithmetic and copies ran while one was open for 5% -> 8% of each run, Pallas kernels for 0% -> 0%
where the time goes in v1:
time: 170 us; the launch traced here: 169 us
  blocking collectives  102 us (60%)
  waiting for transfers between devices  18.1 us (11%)
  other arithmetic  15.1 us (9%)
  starting transfers between devices  13.1 us (8%)
  local copies, waits for them, and re-layouts  12.3 us (7%)
  between operations  4.46 us (3%)
  matrix products  3.64 us (2%)
    psum x4, blocking collectives, broadcast(): return lax.psum(block, axis)  84.6 us
    all_gather x2, blocking collectives, on_device(): north_whole = lax.all_gather(north_below, 'tx', axis=2, tiled=True)  17.9 us
    ppermute x4, waiting for transfers between devices, _turn_lane(): lax.ppermute(carry_out, 'ty', [(dd, dd ^ step_out) for dd in range(e_next)])  8.67 us
    ppermute x4, starting transfers between devices, with_halo(): lax.ppermute(lax.slice_in_dim(block, 0, width, axis=dim), axis, backward)  7.61 us
    ppermute x4, waiting for transfers between devices, with_halo(): lax.ppermute(lax.slice_in_dim(block, block.shape[dim] - width, None, axis...  5.67 us
    unnamed x33, local copies, waits for them, and re-layouts  4.02 us
    ppermute x4, waiting for transfers between devices, with_halo(): lax.ppermute(lax.slice_in_dim(block, 0, width, axis=dim), axis, backward)  3.72 us
    dot_general x2, matrix products, on_device(): jnp.einsum('slm,skyxl->skyxm', vertical_inverse, adjoint, precision=lax.P...  3.64 us
  transfers between devices with their start and end apart: 12, of which 6 were waited for; matrix products, arithmetic and copies ran while one was open for 8% of the time, Pallas kernels for 0%

profile of v1, /device:TPU:0, one launch (start us, length us, event | category | flops | bytes accessed | tf_op | source)
XLA Modules:
  0.0 169.1 jit_solution(7063128167973631640)
XLA Ops:
  0.0 1.4 fusion.41
  3.8 1.9 %fusion.13 = f32[5,3,16,8,128]{4,3,2,1,0:T(8,128)S(1)} fusion(f32[5,3,16,8,128]{4,3,2,1,0:T(8,128)S(1)} %copy-done, f32[5,128,128]{2,1,0:T(8,128)} %param.6), kind=kOutput, calls=%fused_computation.33 | convolution fusion | flops 377487360 | bytes 2293760 | tf_op jit(solution)/shard_map/slm,skyxl->skyxm/dot_general | solution.py:75
  7.8 25.9 %psum.29 = f32[5,1,16,128]{3,2,0,1:T(8,128)S(1)} all-reduce(f32[5,1,16,128]{3,2,0,1:T(8,128)S(1)} %select_bitcast_fusion), channel_id=1, replica_groups=mesh['tx'=8,'ty'=4] {'tx'}, use_global_device_ids=true, to_apply=%region_10.11 | all-reduce | flops 10240 | bytes 81920 | tf_op jit(solution)/shard_map/psum | solution.py:25
  33.7 1.6 collective-permute-start.3
  36.1 2.6 %collective-permute-start = (f32[2,5,3,16,1,128]{5,3,1,4,2,0:T(8,128)}, f32[2,5,3,16,1,128]{5,3,1,4,2,0:T(8,128)}, u32[]{:S(2)}, u32[]{:S(2)}) collective-permute-start(f32[2,5,3,16,1,128]{5,3,1,4,2,0:T(8,128)} %get-tuple-element.33), channel_id=1, source_target_pairs={{4,0},{8,4},{12,8},{16,12},{20,16},{24,20},{28,24},{0,28},{5,1},{9... | collective-permute-start | bytes 737288 | tf_op jit(solution)/shard_map/ppermute | solution.py:18
  40.7 1.5 slice_bitcast_fusion.2
  43.4 18.6 %psum.28 = f32[5,1,8,128]{3,2,0,1:T(8,128)} all-reduce(f32[5,1,8,128]{3,2,0,1:T(8,128)S(1)} %bitcast.179), channel_id=1, replica_groups=mesh['tx'=8,'ty'=4] {'ty'}, use_global_device_ids=true, to_apply=%region_4.5 | all-reduce | flops 5120 | bytes 40960 | tf_op jit(solution)/shard_map/psum | solution.py:25
  62.1 8.5 %all_gather.6 = f32[5,1,64,128]{3,2,0,1:T(8,128)S(1)} all-gather(f32[5,1,8,128]{3,2,0,1:T(8,128)} %psum.28), channel_id=1, replica_groups=mesh['tx'=8,'ty'=4] {'tx'}, dimensions={2}, use_global_device_ids=true | all-gather | bytes 184320 | tf_op jit(solution)/shard_map/all_gather | solution.py:87
  75.9 4.1 %collective-permute-done.4 = f32[5,1,32,128]{3,2,0,1:T(8,128)S(1)} collective-permute-done((f32[5,1,32,128]{3,2,0,1:T(8,128)S(1)}, f32[5,1,32,128]{3,2,0,1:T(8,128)S(1)}, u32[]{:S(2)}, u32[]{:S(2)}) %collective-permute-start.4) | collective-permute-done | bytes 81952 | tf_op jit(solution)/shard_map/ppermute | solution.py:96
  80.1 1.4 pad_maximum_fusion.13
  81.6 2.0 %collective-permute-start.5 = (f32[2,5,3,1,10,128]{5,3,1,4,2,0:T(1,128)S(1)}, f32[2,5,3,1,10,128]{5,3,1,4,2,0:T(1,128)S(1)}, u32[]{:S(2)}, u32[]{:S(2)}) collective-permute-start(f32[2,5,3,1,10,128]{5,3,1,4,2,0:T(1,128)S(1)} %get-tuple-element.25), channel_id=1, source_target_pairs={{0,1},{1,2},{2,3},{3,0},{4,5},{5,6},{6,7},{7,4},{8,9},{9,10},{10,1... | collective-permute-start | bytes 460808 | tf_op jit(solution)/shard_map/ppermute | solution.py:15
  88.4 1.9 %collective-permute-done.5 = f32[2,5,3,1,10,128]{5,3,1,4,2,0:T(1,128)S(1)} collective-permute-done((f32[2,5,3,1,10,128]{5,3,1,4,2,0:T(1,128)S(1)}, f32[2,5,3,1,10,128]{5,3,1,4,2,0:T(1,128)S(1)}, u32[]{:S(2)}, u32[]{:S(2)}) %collective-permute-start.5) | collective-permute-done | bytes 153632 | tf_op jit(solution)/shard_map/ppermute | solution.py:15
  91.1 1.7 %fusion.9 = f32[5,3,16,8,128]{4,3,2,1,0:T(8,128)S(1)} fusion(f32[5,3,16,8,128]{4,2,0,3,1:T(8,128)S(1)} %fusion.5, f32[5,3,16,8,128]{4,3,2,1,0:T(8,128)S(1)} %copy-done.2, f32[5,3,16,8,128]{4,2,0,3,1:T(8,128)S(1)} %fusion.7, f32[5,128,128]{2,1,0:T(8,128)S(1)} %copy-done.10), kind=kOutput, calls=%fused_computation.24 | convolution fusion | flops 378224640 | bytes 4259840 | tf_op jit(solution)/shard_map/slm,skyxl->skyxm/dot_general | solution.py:75
  95.0 1.4 slice_bitcast_fusion
  96.5 17.3 %psum.30 = f32[5,1,8,128]{3,2,0,1:T(8,128)S(1)} all-reduce(f32[5,1,8,128]{3,2,0,1:T(8,128)S(1)} %bitcast.180), channel_id=1, replica_groups=mesh['tx'=8,'ty'=4] {'ty'}, use_global_device_ids=true, to_apply=%region_13.14 | all-reduce | flops 5120 | bytes 40960 | tf_op jit(solution)/shard_map/psum | solution.py:25
  114.6 22.7 %psum.31 = f32[5,1,16,128]{3,2,0,1:T(8,128)S(1)} all-reduce(f32[5,1,16,128]{3,2,0,1:T(8,128)S(1)} %fusion.19), channel_id=1, replica_groups=mesh['tx'=8,'ty'=4] {'tx'}, use_global_device_ids=true, to_apply=%region_16.17 | all-reduce | flops 10240 | bytes 81920 | tf_op jit(solution)/shard_map/psum | solution.py:25
  137.3 9.4 %all_gather.7 = f32[5,1,64,128]{3,2,0,1:T(8,128)S(1)} all-gather(f32[5,1,8,128]{3,2,0,1:T(8,128)S(1)} %psum.30), channel_id=1, replica_groups=mesh['tx'=8,'ty'=4] {'tx'}, dimensions={2}, use_global_device_ids=true | all-gather | bytes 184320 | tf_op jit(solution)/shard_map/all_gather | solution.py:87
  147.1 2.3 %collective-permute-start.6 = (f32[2,5,3,16,1,128]{5,3,2,1,4,0:T(8,128)S(1)}, f32[2,5,3,16,1,128]{5,3,2,1,4,0:T(8,128)S(1)}, u32[]{:S(2)}, u32[]{:S(2)}) collective-permute-start(f32[2,5,3,16,1,128]{5,3,2,1,4,0:T(8,128)S(1)} %get-tuple-element.29), channel_id=1, source_target_pairs={{4,0},{8,4},{12,8},{16,12},{20,16},{24,20},{28,24},{0,28},{5,1},{9... | collective-permute-start | bytes 737288 | tf_op jit(solution)/shard_map/ppermute | solution.py:18
  149.4 1.5 copy.356
  151.8 4.5 %collective-permute-done.10 = f32[5,1,32,128]{3,2,0,1:T(8,128)S(1)} collective-permute-done((f32[5,1,32,128]{3,2,0,1:T(8,128)S(1)}, f32[5,1,32,128]{3,2,0,1:T(8,128)S(1)}, u32[]{:S(2)}, u32[]{:S(2)}) %collective-permute-start.10) | collective-permute-done | bytes 81952 | tf_op jit(solution)/shard_map/ppermute | solution.py:96
  157.0 2.6 %collective-permute-start.8 = (f32[2,5,3,1,10,128]{5,3,2,1,4,0:T(1,128)S(1)}, f32[2,5,3,1,10,128]{5,3,2,1,4,0:T(1,128)S(1)}, u32[]{:S(2)}, u32[]{:S(2)}) collective-permute-start(f32[2,5,3,1,10,128]{5,3,2,1,4,0:T(1,128)S(1)} %get-tuple-element.22), channel_id=1, source_target_pairs={{1,0},{2,1},{3,2},{0,3},{5,4},{6,5},{7,6},{4,7},{9,8},{10,9},{11,1... | collective-permute-start | bytes 460808 | tf_op jit(solution)/shard_map/ppermute | solution.py:18
  159.9 3.0 %collective-permute-done.8 = f32[2,5,3,1,10,128]{5,3,2,1,4,0:T(1,128)S(1)} collective-permute-done((f32[2,5,3,1,10,128]{5,3,2,1,4,0:T(1,128)S(1)}, f32[2,5,3,1,10,128]{5,3,2,1,4,0:T(1,128)S(1)}, u32[]{:S(2)}, u32[]{:S(2)}) %collective-permute-start.8) | collective-permute-done | bytes 153632 | tf_op jit(solution)/shard_map/ppermute | solution.py:18
  162.9 3.8 %collective-permute-done.11 = f32[2,5,3,1,10,128]{5,3,2,1,4,0:T(1,128)S(1)} collective-permute-done((f32[2,5,3,1,10,128]{5,3,2,1,4,0:T(1,128)S(1)}, f32[2,5,3,1,10,128]{5,3,2,1,4,0:T(1,128)S(1)}, u32[]{:S(2)}, u32[]{:S(2)}) %collective-permute-start.11) | collective-permute-done | bytes 153632 | tf_op jit(solution)/shard_map/ppermute | solution.py:15
  167.3 1.8 %fusion.4 = f32[5,3,16,8,128]{4,3,2,1,0:T(8,128)} fusion(f32[5,3,16,8,128]{4,3,2,1,0:T(8,128)S(1)} %copy-done.4, f32[5,3,16,8,128]{4,3,2,1,0:T(8,128)S(1)} %bitcast.162, f32[5,3,16,1,128]{4,3,2,1,0:T(1,128)S(1)} %copy.279, f32[5,3,16,1,128]{4,3,2,1,0:T(1,128)S(1)} %broadcast_select_fusion, f32[5,3,16,8,128]{4,2,1,0,3:T(8,128)S(1)} %fusion), kind=kLoop, calls=%fused_computation.8 | loop fusion | flops 1720320 | bytes 4177920 | tf_op jit(solution)/shard_map/add | solution.py:123
  (108 shorter events, 21.0 us)
Async XLA Ops:
  0.0 3.8 %copy-start = (f32[5,3,16,8,128]{4,3,2,1,0:T(8,128)S(1)}, f32[5,3,16,8,128]{4,3,2,1,0:T(8,128)}, u32[]{:S(2)}) copy-start(f32[5,3,16,8,128]{4,3,2,1,0:T(8,128)} %param.4) | copy-start | bytes 2949124
  6.9 31.9 %copy-start.12 = (s32[40,4]{0,1:T(4,128)S(1)}, s32[40,4]{0,1:T(4,128)}, u32[]{:S(2)}) copy-start(s32[40,4]{0,1:T(4,128)} %param.7) | copy-start | bytes 1924
  33.7 39.8 %collective-permute-start.3 = (f32[5,1,16,128]{3,2,0,1:T(8,128)S(1)}, f32[5,1,16,128]{3,2,0,1:T(8,128)}, u32[]{:S(2)}, u32[]{:S(2)}) collective-permute-start(f32[5,1,16,128]{3,2,0,1:T(8,128)S(1)} %psum.29), channel_id=1, source_target_pairs={{0,1},{1,0},{2,3},{3,2},{4,5},{5,4},{6,7},{7,6},{8,9},{9,8},{10,11... | collective-permute-start | bytes 122888 | tf_op jit(solution)/shard_map/ppermute | solution.py:96
  36.1 44.0 %collective-permute-start.1 = (f32[2,5,3,16,1,128]{5,3,1,4,2,0:T(8,128)}, f32[2,5,3,16,1,128]{5,3,1,4,2,0:T(8,128)}, u32[]{:S(2)}, u32[]{:S(2)}) collective-permute-start(f32[2,5,3,16,1,128]{5,3,1,4,2,0:T(8,128)} %get-tuple-element.32), channel_id=1, source_target_pairs={{0,4},{4,8},{8,12},{12,16},{16,20},{20,24},{24,28},{28,0},{1,5},{5... | collective-permute-start | bytes 737288 | tf_op jit(solution)/shard_map/ppermute | solution.py:15
  36.1 44.0 %collective-permute-start = (f32[2,5,3,16,1,128]{5,3,1,4,2,0:T(8,128)}, f32[2,5,3,16,1,128]{5,3,1,4,2,0:T(8,128)}, u32[]{:S(2)}, u32[]{:S(2)}) collective-permute-start(f32[2,5,3,16,1,128]{5,3,1,4,2,0:T(8,128)} %get-tuple-element.33), channel_id=1, source_target_pairs={{4,0},{8,4},{12,8},{16,12},{20,16},{24,20},{28,24},{0,28},{5,1},{9... | collective-permute-start | bytes 737288 | tf_op jit(solution)/shard_map/ppermute | solution.py:18
  40.7 32.0 %copy-start.8 = (f32[2,3,16,8,128]{4,3,2,1,0:T(8,128)S(1)}, f32[2,3,16,8,128]{4,3,2,1,0:T(8,128)}, u32[]{:S(2)}) copy-start(f32[2,3,16,8,128]{4,3,2,1,0:T(8,128)} %param.5) | copy-start | bytes 1179652
  73.5 17.1 %copy-start.13 = (f32[3]{0:T(128)}, f32[3]{0:T(128)S(1)}, u32[]{:S(2)}) copy-start(f32[3]{0:T(128)S(1)} %neg.19) | copy-start | bytes 40
  74.4 11.2 %copy-start.11 = (f32[5,16,128]{2,1,0:T(8,128)S(1)}, f32[5,16,128]{2,1,0:T(8,128)}, u32[]{:S(2)}) copy-start(f32[5,16,128]{2,1,0:T(8,128)} %dynamic-slice_bitcast_fusion.1) | copy-start | bytes 122884
  74.4 5.7 %collective-permute-start.4 = (f32[5,1,32,128]{3,2,0,1:T(8,128)S(1)}, f32[5,1,32,128]{3,2,0,1:T(8,128)S(1)}, u32[]{:S(2)}, u32[]{:S(2)}) collective-permute-start(f32[5,1,32,128]{3,2,0,1:T(8,128)S(1)} %maximum_select_fusion.1), channel_id=1, source_target_pairs={{0,2},{1,3},{2,0},{3,1},{4,6},{5,7},{6,4},{7,5},{8,10},{9,11},{10,... | collective-permute-start | bytes 245768 | tf_op jit(solution)/shard_map/ppermute | solution.py:96
  80.1 7.5 %copy-start.6 = (f32[5,3,16,8,128]{4,2,0,3,1:T(8,128)S(1)}, f32[5,3,16,8,128]{4,2,0,3,1:T(8,128)}, u32[]{:S(2)}) copy-start(f32[5,3,16,8,128]{4,2,0,3,1:T(8,128)} %get-tuple-element.30) | copy-start | bytes 2949124
  81.5 6.9 %collective-permute-start.2 = (f32[2,5,3,1,10,128]{5,3,1,4,2,0:T(1,128)S(1)}, f32[2,5,3,1,10,128]{5,3,1,4,2,0:T(1,128)S(1)}, u32[]{:S(2)}, u32[]{:S(2)}) collective-permute-start(f32[2,5,3,1,10,128]{5,3,1,4,2,0:T(1,128)S(1)} %get-tuple-element.24), channel_id=1, source_target_pairs={{1,0},{2,1},{3,2},{0,3},{5,4},{6,5},{7,6},{4,7},{9,8},{10,9},{11,1... | collective-permute-start | bytes 460808 | tf_op jit(solution)/shard_map/ppermute | solution.py:18
  81.6 8.8 %collective-permute-start.5 = (f32[2,5,3,1,10,128]{5,3,1,4,2,0:T(1,128)S(1)}, f32[2,5,3,1,10,128]{5,3,1,4,2,0:T(1,128)S(1)}, u32[]{:S(2)}, u32[]{:S(2)}) collective-permute-start(f32[2,5,3,1,10,128]{5,3,1,4,2,0:T(1,128)S(1)} %get-tuple-element.25), channel_id=1, source_target_pairs={{0,1},{1,2},{2,3},{3,0},{4,5},{5,6},{6,7},{7,4},{8,9},{9,10},{10,1... | collective-permute-start | bytes 460808 | tf_op jit(solution)/shard_map/ppermute | solution.py:15
  86.5 4.2 %copy-start.5 = (f32[5,3,16,8,128]{4,2,0,3,1:T(8,128)S(1)}, f32[5,3,16,8,128]{4,2,0,3,1:T(8,128)}, u32[]{:S(2)}) copy-start(f32[5,3,16,8,128]{4,2,0,3,1:T(8,128)} %get-tuple-element.31) | copy-start | bytes 2949124
  87.7 3.4 %copy-start.2 = (f32[5,3,16,8,128]{4,3,2,1,0:T(8,128)S(1)}, f32[5,3,16,8,128]{4,3,2,1,0:T(8,128)}, u32[]{:S(2)}) copy-start(f32[5,3,16,8,128]{4,3,2,1,0:T(8,128)} %copy-done.1) | copy-start | bytes 2949124
  87.7 3.4 %copy-start.10 = (f32[5,128,128]{2,1,0:T(8,128)S(1)}, f32[5,128,128]{2,1,0:T(8,128)}, u32[]{:S(2)}) copy-start(f32[5,128,128]{2,1,0:T(8,128)} %param.6) | copy-start | bytes 983044
  137.3 13.7 %collective-permute-start.9 = (f32[5,1,16,128]{3,2,0,1:T(8,128)S(1)}, f32[5,1,16,128]{3,2,0,1:T(8,128)S(1)}, u32[]{:S(2)}, u32[]{:S(2)}) collective-permute-start(f32[5,1,16,128]{3,2,0,1:T(8,128)S(1)} %psum.31), channel_id=1, source_target_pairs={{0,1},{1,0},{2,3},{3,2},{4,5},{5,4},{6,7},{7,6},{8,9},{9,8},{10,11... | collective-permute-start | bytes 122888 | tf_op jit(solution)/shard_map/ppermute | solution.py:96
  146.7 9.7 %collective-permute-start.7 = (f32[2,5,3,16,1,128]{5,3,1,2,4,0:T(8,128)S(1)}, f32[2,5,3,16,1,128]{5,3,1,2,4,0:T(8,128)S(1)}, u32[]{:S(2)}, u32[]{:S(2)}) collective-permute-start(f32[2,5,3,16,1,128]{5,3,1,2,4,0:T(8,128)S(1)} %copy.298), channel_id=1, source_target_pairs={{0,4},{4,8},{8,12},{12,16},{16,20},{20,24},{24,28},{28,0},{1,5},{5... | collective-permute-start | bytes 737288 | tf_op jit(solution)/shard_map/ppermute | solution.py:15
  147.1 9.3 %collective-permute-start.6 = (f32[2,5,3,16,1,128]{5,3,2,1,4,0:T(8,128)S(1)}, f32[2,5,3,16,1,128]{5,3,2,1,4,0:T(8,128)S(1)}, u32[]{:S(2)}, u32[]{:S(2)}) collective-permute-start(f32[2,5,3,16,1,128]{5,3,2,1,4,0:T(8,128)S(1)} %get-tuple-element.29), channel_id=1, source_target_pairs={{4,0},{8,4},{12,8},{16,12},{20,16},{24,20},{28,24},{0,28},{5,1},{9... | collective-permute-start | bytes 737288 | tf_op jit(solution)/shard_map/ppermute | solution.py:18
  151.0 5.4 %collective-permute-start.10 = (f32[5,1,32,128]{3,2,0,1:T(8,128)S(1)}, f32[5,1,32,128]{3,2,0,1:T(8,128)S(1)}, u32[]{:S(2)}, u32[]{:S(2)}) collective-permute-start(f32[5,1,32,128]{3,2,0,1:T(8,128)S(1)} %maximum_select_fusion.3), channel_id=1, source_target_pairs={{0,2},{1,3},{2,0},{3,1},{4,6},{5,7},{6,4},{7,5},{8,10},{9,11},{10,... | collective-permute-start | bytes 245768 | tf_op jit(solution)/shard_map/ppermute | solution.py:96
  156.7 10.2 %copy-start.7 = (f32[5,3,16,8,128]{4,2,1,0,3:T(8,128)S(1)}, f32[5,3,16,8,128]{4,2,1,0,3:T(8,128)}, u32[]{:S(2)}) copy-start(f32[5,3,16,8,128]{4,2,1,0,3:T(8,128)} %get-tuple-element.26) | copy-start | bytes 2949124
  156.7 10.2 %copy-start.14 = (f32[3]{0:T(128)S(1)}, f32[3]{0:T(128)}, u32[]{:S(2)}) copy-start(f32[3]{0:T(128)} %copy-done.13) | copy-start | bytes 40
  157.0 10.3 %copy-start.4 = (f32[5,3,16,8,128]{4,3,2,1,0:T(8,128)S(1)}, f32[5,3,16,8,128]{4,3,2,1,0:T(8,128)}, u32[]{:S(2)}) copy-start(f32[5,3,16,8,128]{4,3,2,1,0:T(8,128)} %copy-done.3) | copy-start | bytes 2949124
  157.0 5.9 %collective-permute-start.8 = (f32[2,5,3,1,10,128]{5,3,2,1,4,0:T(1,128)S(1)}, f32[2,5,3,1,10,128]{5,3,2,1,4,0:T(1,128)S(1)}, u32[]{:S(2)}, u32[]{:S(2)}) collective-permute-start(f32[2,5,3,1,10,128]{5,3,2,1,4,0:T(1,128)S(1)} %get-tuple-element.22), channel_id=1, source_target_pairs={{1,0},{2,1},{3,2},{0,3},{5,4},{6,5},{7,6},{4,7},{9,8},{10,9},{11,1... | collective-permute-start | bytes 460808 | tf_op jit(solution)/shard_map/ppermute | solution.py:18
  159.6 7.1 %collective-permute-start.11 = (f32[2,5,3,1,10,128]{5,3,2,1,4,0:T(1,128)S(1)}, f32[2,5,3,1,10,128]{5,3,2,1,4,0:T(1,128)S(1)}, u32[]{:S(2)}, u32[]{:S(2)}) collective-permute-start(f32[2,5,3,1,10,128]{5,3,2,1,4,0:T(1,128)S(1)} %get-tuple-element.23), channel_id=1, source_target_pairs={{0,1},{1,2},{2,3},{3,0},{4,5},{5,6},{6,7},{7,4},{8,9},{9,10},{10,1... | collective-permute-start | bytes 460808 | tf_op jit(solution)/shard_map/ppermute | solution.py:15
  (3 other events, 3.7 us)
